TPU v7x, 32 devices: a whole 2x2x4 slice. The times are simulated.
32 devices in a mesh: rep: 8 (over y, x, core), shard: 4 (over z).
Axes of the slice: x: 2, y: 2, z: 4, core: 2. Of those that a mesh axis runs over, the one named last changes fastest.
Arguments:
- gradients: bfloat16 [8, 96, 2560], P(None, 'shard')
- momentum: float32 [8, 96, 2560], P(None, 'shard'), may hold values from -60 to 60
Outputs:
- updates: bfloat16 [8, 96, 2560], P(None, 'shard', 'rep')
- new_momentum: float32 [8, 96, 2560], P(None, 'shard')
All inputs are finite; a program needn't handle non-finite values.
Results may differ from a plain program's by a relative error of at most 0.0014.
Values may be sent and summed in bfloat16 or wider, within the bound.
A program may use at most 64 MiB of HBM per device.

v0:
```python
import math
import jax
import jax.numpy as jnp
from jax import lax
from jax.sharding import PartitionSpec as P

E = 96
D = 2560
ITERS = 5
momentum_decay = 0.95
norm_floor = 1e-07
quintic_terms = (3.4445, -4.775, 2.0315)


def broadcast(x, axis, root):
    mine = lax.axis_index(axis) == root
    return lax.psum(jnp.where(mine, x, jnp.zeros_like(x)), axis)


def batched_schulz(effective):
    totals = jnp.sqrt(jnp.sum(effective * effective, axis=(1, 2), keepdims=True))
    iterate = effective / (totals + norm_floor)
    for turn in range(ITERS):
        gram_mat = jnp.einsum("kij,klj->kil", iterate, iterate, precision=lax.Precision.HIGHEST)
        square_mat = jnp.einsum("kij,kjl->kil", gram_mat, gram_mat, precision=lax.Precision.HIGHEST)
        poly_mat = quintic_terms[1] * gram_mat + quintic_terms[2] * square_mat
        iterate = quintic_terms[0] * iterate + jnp.einsum(
            "kij,kjl->kil", poly_mat, iterate, precision=lax.Precision.HIGHEST
        )
    return iterate


def per_device(gradients, momentum):
    update_scale = 0.2 * math.sqrt(max(E, D))
    gradient_values = gradients.astype(jnp.float32)
    new_momentum = momentum_decay * momentum + gradient_values
    effective_rows = gradient_values + momentum_decay * new_momentum
    effective = lax.all_to_all(effective_rows, "shard", split_axis=0, concat_axis=1, tiled=True)
    slot_count = effective.shape[0]
    replicas = lax.axis_size("rep")
    column = lax.axis_index("shard")
    replica = lax.axis_index("rep")
    slot_owners = (column * slot_count + jnp.arange(slot_count, dtype=jnp.int32)) % replicas
    owned = slot_owners == replica

    def compute_update(operand):
        return (update_scale * batched_schulz(operand)).astype(jnp.bfloat16)

    def skip_update(operand):
        return jnp.zeros(operand.shape, jnp.bfloat16)

    local_updates = lax.cond(jnp.any(owned), compute_update, skip_update, effective)
    copies = []
    for slot_index in range(slot_count):
        copies.append(broadcast(local_updates[slot_index], "rep", slot_owners[slot_index]))
    stacked = jnp.stack(copies)
    result_rows = lax.all_to_all(stacked, "shard", split_axis=1, concat_axis=0, tiled=True)
    col_width = result_rows.shape[2] // replicas
    kept_cols = lax.dynamic_slice_in_dim(result_rows, replica * col_width, col_width, 2)
    return (kept_cols, new_momentum)


def solution(mesh):
    in_specs = (P(None, "shard", None), P(None, "shard", None))
    out_specs = (P(None, "shard", "rep"), P(None, "shard", None))
    return jax.shard_map(
        per_device, mesh=mesh, in_specs=in_specs, out_specs=out_specs, check_vma=False
    )
```

profile of v0, /device:TPU:0, one launch (start us, length us, event | category | flops | bytes accessed | tf_op | source)
XLA Modules:
  0.0 180.7 jit_solution(16023603056860702382)
XLA Ops:
  7.2 4.4 %convert_add_fusion = (f32[8,24,2560]{2,1,0:T(8,128)}, f32[8,24,2560]{2,1,0:T(8,128)}) fusion(bf16[8,24,2560]{2,1,0:T(8,128)(2,1)} %param.4, f32[8,24,2560]{2,1,0:T(8,128)} %param.5), kind=kLoop, calls=%fused_computation.22 | loop fusion | flops 2457600 | bytes 6881280 | tf_op jit(solution)/shard_map/add | solution.py:37
  11.5 6.3 %all-to-all-start = ((f32[8,24,2560]{2,1,0:T(8,128)}), f32[8,24,2560]{2,1,0:T(8,128)S(1)}, u32[]{:S(2)}, u32[]{:S(2)}) async-start(f32[8,24,2560]{2,1,0:T(8,128)} %get-tuple-element.20), calls=%async_computation | async-start | bytes 3932160 | tf_op jit(solution)/shard_map/all_to_all | solution.py:38
  17.8 0.0 all-reduce.3.cloned.1.call-start
  17.8 0.6 compare_reduce_fusion
  19.2 0.6 fusion.8
  20.9 42.3 %all-to-all-done = f32[8,24,2560]{2,1,0:T(8,128)S(1)} async-done(((f32[8,24,2560]{2,1,0:T(8,128)}), f32[8,24,2560]{2,1,0:T(8,128)S(1)}, u32[]{:S(2)}, u32[]{:S(2)}) %all-to-all-start) | async-done | bytes 1966112 | tf_op jit(solution)/shard_map/all_to_all | solution.py:38
  63.2 0.1 copy.13
  63.4 21.7 %conditional.1 = (bf16[96,2560]{1,0:T(8,128)(2,1)S(1)}, bf16[96,2560]{1,0:T(8,128)(2,1)S(1)}) conditional(s32[]{:T(128)} %convert_element_type.10, () %tuple.22, f32[2,4,24,2560]{3,2,1,0:T(8,128)S(1)} %bitcast.50), branch_computations={%region_1.2_spmd, %region_2.4_spmd} | conditional | flops 5776128000 | bytes 37847088 | solution.py:52
  63.4 0.4 multiply_reduce_fusion
  63.8 0.3 bitcast_divide_fusion
  64.1 1.9 %fusion.9 = f32[2,96,96]{2,1,0:T(8,128)S(1)} fusion(f32[2,96,2560]{2,1,0:T(8,128)S(1)} %bitcast_divide_fusion), kind=kOutput, calls=%fused_computation.35 | convolution fusion | flops 566231040 | bytes 2039808 | tf_op jit(solution)/shard_map/cond/branch_1_fun/kij,klj->kil/dot_general | solution.py:24
  66.0 0.2 fusion.2
  66.2 1.9 %convolution_add_fusion.4 = f32[2,96,2560]{2,1,0:T(8,128)S(1)} fusion(f32[2,96,96]{2,1,0:T(8,128)S(1)} %fusion.2, f32[2,96,2560]{2,1,0:T(8,128)S(1)} %bitcast_divide_fusion), kind=kOutput, calls=%fused_computation.5 | convolution fusion | flops 567214080 | bytes 4005888 | tf_op jit(solution)/shard_map/cond/branch_1_fun/kij,kjl->kil/dot_general | solution.py:27
  68.2 1.9 %fusion.10 = f32[2,96,96]{2,1,0:T(8,128)S(1)} fusion(f32[2,96,2560]{2,1,0:T(8,128)S(1)} %convolution_add_fusion.4), kind=kOutput, calls=%fused_computation.36 | convolution fusion | flops 566231040 | bytes 2039808 | tf_op jit(solution)/shard_map/cond/branch_1_fun/kij,klj->kil/dot_general | solution.py:24
  70.1 0.2 fusion.3
  70.3 1.9 %convolution_add_fusion.3 = f32[2,96,2560]{2,1,0:T(8,128)S(1)} fusion(f32[2,96,96]{2,1,0:T(8,128)S(1)} %fusion.3, f32[2,96,2560]{2,1,0:T(8,128)S(1)} %convolution_add_fusion.4), kind=kOutput, calls=%fused_computation.4 | convolution fusion | flops 567214080 | bytes 4005888 | tf_op jit(solution)/shard_map/cond/branch_1_fun/kij,kjl->kil/dot_general | solution.py:27
  72.3 1.9 %fusion.11 = f32[2,96,96]{2,1,0:T(8,128)S(1)} fusion(f32[2,96,2560]{2,1,0:T(8,128)S(1)} %convolution_add_fusion.3), kind=kOutput, calls=%fused_computation.37 | convolution fusion | flops 566231040 | bytes 2039808 | tf_op jit(solution)/shard_map/cond/branch_1_fun/kij,klj->kil/dot_general | solution.py:24
  74.2 0.2 fusion.4
  74.4 1.9 %convolution_add_fusion.2 = f32[2,96,2560]{2,1,0:T(8,128)S(1)} fusion(f32[2,96,96]{2,1,0:T(8,128)S(1)} %fusion.4, f32[2,96,2560]{2,1,0:T(8,128)S(1)} %convolution_add_fusion.3), kind=kOutput, calls=%fused_computation.3 | convolution fusion | flops 567214080 | bytes 4005888 | tf_op jit(solution)/shard_map/cond/branch_1_fun/kij,kjl->kil/dot_general | solution.py:27
  76.4 2.1 %fusion.12 = f32[2,96,96]{2,1,0:T(8,128)S(1)} fusion(f32[2,96,2560]{2,1,0:T(8,128)S(1)} %convolution_add_fusion.2), kind=kOutput, calls=%fused_computation.38 | convolution fusion | flops 566231040 | bytes 2039808 | tf_op jit(solution)/shard_map/cond/branch_1_fun/kij,klj->kil/dot_general | solution.py:24
  78.4 0.2 fusion.5
  78.7 1.9 %convolution_add_fusion.1 = f32[2,96,2560]{2,1,0:T(8,128)S(1)} fusion(f32[2,96,96]{2,1,0:T(8,128)S(1)} %fusion.5, f32[2,96,2560]{2,1,0:T(8,128)S(1)} %convolution_add_fusion.2), kind=kOutput, calls=%fused_computation.2 | convolution fusion | flops 567214080 | bytes 4005888 | tf_op jit(solution)/shard_map/cond/branch_1_fun/kij,kjl->kil/dot_general | solution.py:27
  80.6 1.9 %fusion.13 = f32[2,96,96]{2,1,0:T(8,128)S(1)} fusion(f32[2,96,2560]{2,1,0:T(8,128)S(1)} %convolution_add_fusion.1), kind=kOutput, calls=%fused_computation.39 | convolution fusion | flops 566231040 | bytes 2039808 | tf_op jit(solution)/shard_map/cond/branch_1_fun/kij,klj->kil/dot_general | solution.py:24
  82.5 0.2 fusion.6
  82.8 2.0 %fusion.1 = bf16[2,96,2560]{2,1,0:T(8,128)(2,1)S(1)} fusion(f32[2,96,96]{2,1,0:T(8,128)S(1)} %fusion.6, f32[2,96,2560]{2,1,0:T(8,128)S(1)} %convolution_add_fusion.1), kind=kOutput, calls=%fused_computation.6 | convolution fusion | flops 568197120 | bytes 3022848 | tf_op jit(solution)/shard_map/cond/branch_1_fun/kij,kjl->kil/dot_general | solution.py:27
  84.8 0.1 slice_bitcast_fusion
  85.1 1.1 select_bitcast_fusion
  86.2 0.0 all-reduce.3.cloned.1.call-update
  86.2 55.7 %all-reduce.3.cloned.1.call-done = (bf16[1,96,2560]{2,1,0:T(8,128)(2,1)}, bf16[1,96,2560]{2,1,0:T(8,128)(2,1)}) async-done(((bf16[1,96,2560]{2,1,0:T(8,128)(2,1)}, bf16[1,96,2560]{2,1,0:T(8,128)(2,1)}), (bf16[1,96,2560]{2,1,0:T(8,128)(2,1)}, bf16[1,96,2560]{2,1,0:T(8,128)(2,1)})) %all-reduce.3.cloned.1.call-update) | async-done | bytes 983056 | tf_op jit(solution)/shard_map/psum | solution.py:17
  141.8 1.3 pad_maximum_fusion
  143.1 2.0 %copy.10 = bf16[2,96,2560]{2,0,1:T(2,128)(2,1)} copy(bf16[2,96,2560]{2,1,0:T(8,128)(2,1)S(1)} %pad_maximum_fusion) | data formatting | bytes 1966080 | tf_op jit(solution)/shard_map/stack | solution.py:56
  145.1 4.4 %all-to-all-start.1 = ((bf16[2,96,2560]{2,0,1:T(2,128)(2,1)}), bf16[2,96,2560]{2,0,1:T(2,128)(2,1)S(1)}, u32[]{:S(2)}, u32[]{:S(2)}) async-start(bf16[2,96,2560]{2,0,1:T(2,128)(2,1)} %copy.10), calls=%async_computation.1 | async-start | bytes 1966080 | tf_op jit(solution)/shard_map/all_to_all | solution.py:57
  149.5 23.4 %all-to-all-done.1 = bf16[2,96,2560]{2,0,1:T(2,128)(2,1)S(1)} async-done(((bf16[2,96,2560]{2,0,1:T(2,128)(2,1)}), bf16[2,96,2560]{2,0,1:T(2,128)(2,1)S(1)}, u32[]{:S(2)}, u32[]{:S(2)}) %all-to-all-start.1) | async-done | bytes 983072 | tf_op jit(solution)/shard_map/all_to_all | solution.py:57
  173.0 0.1 copy.11
  173.1 0.8 constant_dynamic-slice_fusion
  (2 shorter events, 0.0 us)
Async XLA Ops:
  11.5 51.7 %all-to-all-start = ((f32[8,24,2560]{2,1,0:T(8,128)}), f32[8,24,2560]{2,1,0:T(8,128)S(1)}, u32[]{:S(2)}, u32[]{:S(2)}) async-start(f32[8,24,2560]{2,1,0:T(8,128)} %get-tuple-element.20), calls=%async_computation | async-start | bytes 3932160 | tf_op jit(solution)/shard_map/all_to_all | solution.py:38
  17.8 124.0 %all-reduce.3.cloned.1.call-start = ((), (), s32[]{:S(2)}) async-start(), calls=%async_computation.2 | async-start | bytes 1966080 | tf_op jit(solution)/shard_map/psum | solution.py:17
  145.1 27.9 %all-to-all-start.1 = ((bf16[2,96,2560]{2,0,1:T(2,128)(2,1)}), bf16[2,96,2560]{2,0,1:T(2,128)(2,1)S(1)}, u32[]{:S(2)}, u32[]{:S(2)}) async-start(bf16[2,96,2560]{2,0,1:T(2,128)(2,1)} %copy.10), calls=%async_computation.1 | async-start | bytes 1966080 | tf_op jit(solution)/shard_map/all_to_all | solution.py:57
Sparse Core Ops, SparseCore 0:
  86.3 55.4 all-reduce.2
where the time goes:
time: 181 us
  waiting for transfers between devices  121 us (67%)
  matrix products  20.6 us (11%)
  between operations  15.9 us (9%)
  starting transfers between devices  10.8 us (6%)
  other arithmetic  8.01 us (4%)
  local copies, waits for them, and re-layouts  3.64 us (2%)
    psum x1, waiting for transfers between devices, broadcast(): return lax.psum(jnp.where(mine, x, jnp.zeros_like(x)), axis)  55.7 us
    all_to_all x1, waiting for transfers between devices, per_device(): lax.all_to_all(effective_rows, 'shard', split_axis=0, concat_axis=1, tile...  42.3 us
    all_to_all x1, waiting for transfers between devices, per_device(): lax.all_to_all(stacked, 'shard', split_axis=1, concat_axis=0, tiled=True)  23.4 us
    dot_general x5, matrix products, batched_schulz(): jnp.einsum('kij,kjl->kil', poly_mat, iterate, precision=lax.Precision.HIG...  9.76 us
    dot_general x5, matrix products, batched_schulz(): jnp.einsum('kij,klj->kil', iterate, iterate, precision=lax.Precision.HIGH...  9.67 us
    all_to_all x1, starting transfers between devices, per_device(): lax.all_to_all(effective_rows, 'shard', split_axis=0, concat_axis=1, tile...  6.32 us
    all_to_all x1, starting transfers between devices, per_device(): lax.all_to_all(stacked, 'shard', split_axis=1, concat_axis=0, tiled=True)  4.45 us
    add x1, other arithmetic, per_device(): effective_rows = gradient_values + momentum_decay * new_momentum  4.36 us
  transfers between devices with their start and end apart: 3, of which 3 were waited for; matrix products, arithmetic and copies ran while one was open for 1% of the time, Pallas kernels for 0%

commit v1 on v0

--- a/solution.py
+++ b/solution.py
@@ -1,3 +1,4 @@
+import functools
 import math
 import jax
 import jax.numpy as jnp
@@ -10,6 +11,24 @@
 momentum_decay = 0.95
 norm_floor = 1e-07
 quintic_terms = (3.4445, -4.775, 2.0315)
+
+
+def tell_the_table(tile_in, axis_name):
+    long_array, fresh = (lax.axis_size(axis_name), lax.axis_index(axis_name))
+    last = tile_in.shape[1] // long_array
+    y = jnp.roll(tile_in, -fresh * last, axis=1)
+    parts_seen = [lax.slice_in_dim(y, 0, last, axis=1)]
+    for i in range(1, long_array):
+        reached = lax.slice_in_dim(y, i * last, (i + 1) * last, axis=1)
+        prior = lax.ppermute(
+            reached, axis_name, [(pp, (pp + i) % long_array) for pp in range(long_array)]
+        )
+        parts_seen.append(prior)
+    carry = jnp.concatenate(parts_seen[::-1], axis=0)
+    return jnp.roll(carry, shift=(fresh + 1) * parts_seen[0].shape[0], axis=0)
+
+
+step_on_lane = functools.partial(tell_the_table, axis_name="shard")
 
 
 def broadcast(x, axis, root):
@@ -54,7 +73,7 @@
     for slot_index in range(slot_count):
         copies.append(broadcast(local_updates[slot_index], "rep", slot_owners[slot_index]))
     stacked = jnp.stack(copies)
-    result_rows = lax.all_to_all(stacked, "shard", split_axis=1, concat_axis=0, tiled=True)
+    result_rows = step_on_lane(stacked)
     col_width = result_rows.shape[2] // replicas
     kept_cols = lax.dynamic_slice_in_dim(result_rows, replica * col_width, col_width, 2)
     return (kept_cols, new_momentum)

time: 181 us -> 175 us (0.967)
  waiting for transfers between devices: 121 us -> 117 us
  local copies, waits for them, and re-layouts: 3.64 us -> 1.76 us
    all_to_all x1 -> x0, waiting for transfers between devices: 23.4 us -> none  [per_device(): lax.all_to_all(stacked, 'shard', split_axis=1, concat_axis=0, tiled=True)]
    ppermute x0 -> x3, waiting for transfers between devices: none -> 19 us  [tell_the_table(): lax.ppermute(reached, axis_name, [(pp, (pp + i) % long_array) for pp in r...]
    all_to_all x1 -> x0, starting transfers between devices: 4.45 us -> none  [per_device(): lax.all_to_all(stacked, 'shard', split_axis=1, concat_axis=0, tiled=True)]
    ppermute x0 -> x3, starting transfers between devices: none -> 4.4 us  [tell_the_table(): lax.ppermute(reached, axis_name, [(pp, (pp + i) % long_array) for pp in r...]
    another operation x1 -> x0, local copies, waits for them, and re-layouts: 1.97 us -> none  [per_device(): stacked = jnp.stack(copies)]
    concatenate x0 -> x1, other arithmetic: none -> 1.83 us  [tell_the_table(): y = jnp.roll(tile_in, -fresh * last, axis=1)]
  transfers between devices with their start and end apart: 3 -> 5, of which waited for: 3 -> 4; matrix products, arithmetic and copies ran while one was open for 1% -> 1% of each run, Pallas kernels for 0% -> 0%
where the time goes in v1:
time: 175 us
  waiting for transfers between devices  117 us (67%)
  matrix products  20.6 us (12%)
  between operations  16.1 us (9%)
  starting transfers between devices  10.7 us (6%)
  other arithmetic  8.59 us (5%)
  local copies, waits for them, and re-layouts  1.76 us (1%)
    psum x1, waiting for transfers between devices, broadcast(): return lax.psum(jnp.where(mine, x, jnp.zeros_like(x)), axis)  55.6 us
    all_to_all x1, waiting for transfers between devices, per_device(): lax.all_to_all(effective_rows, 'shard', split_axis=0, concat_axis=1, tile...  42.2 us
    ppermute x3, waiting for transfers between devices, tell_the_table(): lax.ppermute(reached, axis_name, [(pp, (pp + i) % long_array) for pp in r...  19 us
    dot_general x5, matrix products, batched_schulz(): jnp.einsum('kij,kjl->kil', poly_mat, iterate, precision=lax.Precision.HIG...  9.76 us
    dot_general x5, matrix products, batched_schulz(): jnp.einsum('kij,klj->kil', iterate, iterate, precision=lax.Precision.HIGH...  9.67 us
    all_to_all x1, starting transfers between devices, per_device(): lax.all_to_all(effective_rows, 'shard', split_axis=0, concat_axis=1, tile...  6.32 us
    ppermute x3, starting transfers between devices, tell_the_table(): lax.ppermute(reached, axis_name, [(pp, (pp + i) % long_array) for pp in r...  4.4 us
    add x1, other arithmetic, per_device(): effective_rows = gradient_values + momentum_decay * new_momentum  4.37 us
  transfers between devices with their start and end apart: 5, of which 4 were waited for; matrix products, arithmetic and copies ran while one was open for 1% of the time, Pallas kernels for 0%

profile of v1, /device:TPU:0, one launch (start us, length us, event | category | flops | bytes accessed | tf_op | source)
XLA Modules:
  0.0 175.0 jit_solution(11043039784954570169)
XLA Ops:
  7.2 4.4 %convert_add_fusion = (f32[8,24,2560]{2,1,0:T(8,128)}, f32[8,24,2560]{2,1,0:T(8,128)}) fusion(bf16[8,24,2560]{2,1,0:T(8,128)(2,1)} %param.4, f32[8,24,2560]{2,1,0:T(8,128)} %param.5), kind=kLoop, calls=%fused_computation.22 | loop fusion | flops 2457600 | bytes 6881280 | tf_op jit(solution)/shard_map/add | solution.py:56
  11.5 6.3 %all-to-all-start = ((f32[8,24,2560]{2,1,0:T(8,128)}), f32[8,24,2560]{2,1,0:T(8,128)S(1)}, u32[]{:S(2)}, u32[]{:S(2)}) async-start(f32[8,24,2560]{2,1,0:T(8,128)} %get-tuple-element.20), calls=%async_computation | async-start | bytes 3932160 | tf_op jit(solution)/shard_map/all_to_all | solution.py:57
  17.9 0.0 all-reduce.3.cloned.1.call-start
  17.9 0.6 compare_reduce_fusion
  19.2 0.6 fusion.12
  21.0 42.2 %all-to-all-done = f32[8,24,2560]{2,1,0:T(8,128)S(1)} async-done(((f32[8,24,2560]{2,1,0:T(8,128)}), f32[8,24,2560]{2,1,0:T(8,128)S(1)}, u32[]{:S(2)}, u32[]{:S(2)}) %all-to-all-start) | async-done | bytes 1966112 | tf_op jit(solution)/shard_map/all_to_all | solution.py:57
  63.2 0.1 copy.6
  63.4 21.7 %conditional.1 = (bf16[96,2560]{1,0:T(8,128)(2,1)S(1)}, bf16[96,2560]{1,0:T(8,128)(2,1)S(1)}) conditional(s32[]{:T(128)} %convert_element_type.10, () %tuple.22, f32[2,4,24,2560]{3,2,1,0:T(8,128)S(1)} %bitcast.46), branch_computations={%region_1.2_spmd, %region_2.4_spmd} | conditional | flops 5776128000 | bytes 37847088 | solution.py:71
  63.4 0.4 multiply_reduce_fusion
  63.8 0.3 bitcast_divide_fusion
  64.1 1.9 %fusion.13 = f32[2,96,96]{2,1,0:T(8,128)S(1)} fusion(f32[2,96,2560]{2,1,0:T(8,128)S(1)} %bitcast_divide_fusion), kind=kOutput, calls=%fused_computation.50 | convolution fusion | flops 566231040 | bytes 2039808 | tf_op jit(solution)/shard_map/cond/branch_1_fun/kij,klj->kil/dot_general | solution.py:43
  66.0 0.2 fusion.2
  66.2 1.9 %convolution_add_fusion.4 = f32[2,96,2560]{2,1,0:T(8,128)S(1)} fusion(f32[2,96,96]{2,1,0:T(8,128)S(1)} %fusion.2, f32[2,96,2560]{2,1,0:T(8,128)S(1)} %bitcast_divide_fusion), kind=kOutput, calls=%fused_computation.5 | convolution fusion | flops 567214080 | bytes 4005888 | tf_op jit(solution)/shard_map/cond/branch_1_fun/kij,kjl->kil/dot_general | solution.py:46
  68.2 1.9 %fusion.14 = f32[2,96,96]{2,1,0:T(8,128)S(1)} fusion(f32[2,96,2560]{2,1,0:T(8,128)S(1)} %convolution_add_fusion.4), kind=kOutput, calls=%fused_computation.51 | convolution fusion | flops 566231040 | bytes 2039808 | tf_op jit(solution)/shard_map/cond/branch_1_fun/kij,klj->kil/dot_general | solution.py:43
  70.1 0.2 fusion.3
  70.3 1.9 %convolution_add_fusion.3 = f32[2,96,2560]{2,1,0:T(8,128)S(1)} fusion(f32[2,96,96]{2,1,0:T(8,128)S(1)} %fusion.3, f32[2,96,2560]{2,1,0:T(8,128)S(1)} %convolution_add_fusion.4), kind=kOutput, calls=%fused_computation.4 | convolution fusion | flops 567214080 | bytes 4005888 | tf_op jit(solution)/shard_map/cond/branch_1_fun/kij,kjl->kil/dot_general | solution.py:46
  72.3 1.9 %fusion.15 = f32[2,96,96]{2,1,0:T(8,128)S(1)} fusion(f32[2,96,2560]{2,1,0:T(8,128)S(1)} %convolution_add_fusion.3), kind=kOutput, calls=%fused_computation.52 | convolution fusion | flops 566231040 | bytes 2039808 | tf_op jit(solution)/shard_map/cond/branch_1_fun/kij,klj->kil/dot_general | solution.py:43
  74.2 0.2 fusion.4
  74.4 1.9 %convolution_add_fusion.2 = f32[2,96,2560]{2,1,0:T(8,128)S(1)} fusion(f32[2,96,96]{2,1,0:T(8,128)S(1)} %fusion.4, f32[2,96,2560]{2,1,0:T(8,128)S(1)} %convolution_add_fusion.3), kind=kOutput, calls=%fused_computation.3 | convolution fusion | flops 567214080 | bytes 4005888 | tf_op jit(solution)/shard_map/cond/branch_1_fun/kij,kjl->kil/dot_general | solution.py:46
  76.4 2.1 %fusion.16 = f32[2,96,96]{2,1,0:T(8,128)S(1)} fusion(f32[2,96,2560]{2,1,0:T(8,128)S(1)} %convolution_add_fusion.2), kind=kOutput, calls=%fused_computation.53 | convolution fusion | flops 566231040 | bytes 2039808 | tf_op jit(solution)/shard_map/cond/branch_1_fun/kij,klj->kil/dot_general | solution.py:43
  78.5 0.2 fusion.5
  78.7 1.9 %convolution_add_fusion.1 = f32[2,96,2560]{2,1,0:T(8,128)S(1)} fusion(f32[2,96,96]{2,1,0:T(8,128)S(1)} %fusion.5, f32[2,96,2560]{2,1,0:T(8,128)S(1)} %convolution_add_fusion.2), kind=kOutput, calls=%fused_computation.2 | convolution fusion | flops 567214080 | bytes 4005888 | tf_op jit(solution)/shard_map/cond/branch_1_fun/kij,kjl->kil/dot_general | solution.py:46
  80.7 1.9 %fusion.17 = f32[2,96,96]{2,1,0:T(8,128)S(1)} fusion(f32[2,96,2560]{2,1,0:T(8,128)S(1)} %convolution_add_fusion.1), kind=kOutput, calls=%fused_computation.54 | convolution fusion | flops 566231040 | bytes 2039808 | tf_op jit(solution)/shard_map/cond/branch_1_fun/kij,klj->kil/dot_general | solution.py:43
  82.6 0.2 fusion.6
  82.8 2.0 %fusion.1 = bf16[2,96,2560]{2,1,0:T(8,128)(2,1)S(1)} fusion(f32[2,96,96]{2,1,0:T(8,128)S(1)} %fusion.6, f32[2,96,2560]{2,1,0:T(8,128)S(1)} %convolution_add_fusion.1), kind=kOutput, calls=%fused_computation.6 | convolution fusion | flops 568197120 | bytes 3022848 | tf_op jit(solution)/shard_map/cond/branch_1_fun/kij,kjl->kil/dot_general | solution.py:46
  84.8 0.1 slice_bitcast_fusion
  85.1 1.1 select_bitcast_fusion
  86.2 0.0 all-reduce.3.cloned.1.call-update
  86.2 55.6 %all-reduce.3.cloned.1.call-done = (bf16[1,96,2560]{2,1,0:T(8,128)(2,1)}, bf16[1,96,2560]{2,1,0:T(8,128)(2,1)}) async-done(((bf16[1,96,2560]{2,1,0:T(8,128)(2,1)}, bf16[1,96,2560]{2,1,0:T(8,128)(2,1)}), (bf16[1,96,2560]{2,1,0:T(8,128)(2,1)}, bf16[1,96,2560]{2,1,0:T(8,128)(2,1)})) %all-reduce.3.cloned.1.call-update) | async-done | bytes 983056 | tf_op jit(solution)/shard_map/psum | solution.py:36
  141.9 1.8 %fusion.8 = bf16[2,96,2560]{2,1,0:T(8,128)(2,1)S(1)} fusion(s32[]{:T(128)S(6)} %select_n.56, bf16[1,96,2560]{2,1,0:T(8,128)(2,1)} %get-tuple-element.18, bf16[1,96,2560]{2,1,0:T(8,128)(2,1)} %get-tuple-element.19), kind=kLoop, calls=%fused_computation.30 | loop fusion | flops 3932160 | bytes 1966084 | tf_op jit(solution)/shard_map/jit(_roll_dynamic)/concatenate | solution.py:19
  143.7 0.1 fusion.11
  143.7 3.3 %collective-permute-start = (bf16[2,24,2560]{2,1,0:T(8,128)(2,1)S(1)}, bf16[2,24,2560]{2,1,0:T(8,128)(2,1)S(1)}, u32[]{:S(2)}, u32[]{:S(2)}) collective-permute-start(bf16[2,24,2560]{2,1,0:T(8,128)(2,1)S(1)} %get-tuple-element.26), channel_id=1, source_target_pairs={{0,3},{1,0},{2,1},{3,2},{4,7},{5,4},{6,5},{7,6},{8,11},{9,8},{10,9... | collective-permute-start | bytes 737288 | tf_op jit(solution)/shard_map/ppermute | solution.py:23
  147.0 0.0 collective-permute-start.1
  147.0 1.1 collective-permute-start.2
  148.1 5.3 %collective-permute-done = bf16[2,24,2560]{2,1,0:T(8,128)(2,1)S(1)} collective-permute-done((bf16[2,24,2560]{2,1,0:T(8,128)(2,1)S(1)}, bf16[2,24,2560]{2,1,0:T(8,128)(2,1)S(1)}, u32[]{:S(2)}, u32[]{:S(2)}) %collective-permute-start) | collective-permute-done | bytes 245792 | tf_op jit(solution)/shard_map/ppermute | solution.py:23
  153.5 13.7 %collective-permute-done.1 = bf16[2,24,2560]{2,1,0:T(8,128)(2,1)S(1)} collective-permute-done((bf16[2,24,2560]{2,1,0:T(8,128)(2,1)S(1)}, bf16[2,24,2560]{2,1,0:T(8,128)(2,1)S(1)}, u32[]{:S(2)}, u32[]{:S(2)}) %collective-permute-start.1) | collective-permute-done | bytes 245792 | tf_op jit(solution)/shard_map/ppermute | solution.py:23
  167.2 0.0 collective-permute-done.2
  167.4 0.8 constant_dynamic-slice_fusion
  (10 shorter events, 0.2 us)
Async XLA Ops:
  11.5 51.7 %all-to-all-start = ((f32[8,24,2560]{2,1,0:T(8,128)}), f32[8,24,2560]{2,1,0:T(8,128)S(1)}, u32[]{:S(2)}, u32[]{:S(2)}) async-start(f32[8,24,2560]{2,1,0:T(8,128)} %get-tuple-element.20), calls=%async_computation | async-start | bytes 3932160 | tf_op jit(solution)/shard_map/all_to_all | solution.py:57
  17.9 124.0 %all-reduce.3.cloned.1.call-start = ((), (), s32[]{:S(2)}) async-start(), calls=%async_computation.1 | async-start | bytes 1966080 | tf_op jit(solution)/shard_map/psum | solution.py:36
  143.7 9.7 %collective-permute-start = (bf16[2,24,2560]{2,1,0:T(8,128)(2,1)S(1)}, bf16[2,24,2560]{2,1,0:T(8,128)(2,1)S(1)}, u32[]{:S(2)}, u32[]{:S(2)}) collective-permute-start(bf16[2,24,2560]{2,1,0:T(8,128)(2,1)S(1)} %get-tuple-element.26), channel_id=1, source_target_pairs={{0,3},{1,0},{2,1},{3,2},{4,7},{5,4},{6,5},{7,6},{8,11},{9,8},{10,9... | collective-permute-start | bytes 737288 | tf_op jit(solution)/shard_map/ppermute | solution.py:23
  147.0 20.2 %collective-permute-start.1 = (bf16[2,24,2560]{2,1,0:T(8,128)(2,1)S(1)}, bf16[2,24,2560]{2,1,0:T(8,128)(2,1)S(1)}, u32[]{:S(2)}, u32[]{:S(2)}) collective-permute-start(bf16[2,24,2560]{2,1,0:T(8,128)(2,1)S(1)} %get-tuple-element.25), channel_id=1, source_target_pairs={{0,2},{1,3},{2,0},{3,1},{4,6},{5,7},{6,4},{7,5},{8,10},{9,11},{10,... | collective-permute-start | bytes 737288 | tf_op jit(solution)/shard_map/ppermute | solution.py:23
  147.0 20.2 %collective-permute-start.2 = (bf16[2,24,2560]{2,1,0:T(8,128)(2,1)S(1)}, bf16[2,24,2560]{2,1,0:T(8,128)(2,1)S(1)}, u32[]{:S(2)}, u32[]{:S(2)}) collective-permute-start(bf16[2,24,2560]{2,1,0:T(8,128)(2,1)S(1)} %get-tuple-element.24), channel_id=1, source_target_pairs={{0,1},{1,2},{2,3},{3,0},{4,5},{5,6},{6,7},{7,4},{8,9},{9,10},{10,1... | collective-permute-start | bytes 737288 | tf_op jit(solution)/shard_map/ppermute | solution.py:23
Sparse Core Ops, SparseCore 0:
  86.3 55.4 all-reduce.2
